TPU v7x, 512 devices: a whole 4x8x8 slice. The times are simulated.
512 devices in a mesh: gy: 4 (over z_hi, core), gx: 4 (over z_lo), dp: 32 (over x, y).
Axes of the slice: x: 4, y: 8, z: 8 (z_hi: 2, z_lo: 4; z = z_hi * 4 + z_lo), core: 2. Of those that a mesh axis runs over, the one named last changes fastest.
Arguments:
- tokens: bfloat16 [32, 4, 4, 128, 512], P('dp', 'gy', 'gx'), may hold values from -6 to 6
- tile_ids: int32 [32, 4, 4, 2], P('dp'), may hold values from -1 to 15, as said below
- w_qkv: bfloat16 [512, 768], P('dp'), may hold values from -0.25 to 0.25
- w_out: bfloat16 [256, 512], P('dp'), may hold values from -0.75 to 0.75
- norm_gain: float32 [512], replicated, may hold values from 0.1 to 1.9
- rel_bias: float32 [8, 49], replicated, may hold values from -2 to 304
- update_grad: bfloat16 [32, 4, 4, 128, 512], P('dp', 'gy', 'gx'), may hold values from -6 to 6
Outputs:
- update: bfloat16 [32, 4, 4, 128, 512], P('dp', 'gy', 'gx')
- grad_tokens: bfloat16 [32, 4, 4, 128, 512], P('dp', 'gy', 'gx')
- grad_qkv: float32 [512, 768], P('dp')
- grad_out: float32 [256, 512], P('dp')
- grad_gain: float32 [512], replicated
- grad_bias: float32 [8, 49], replicated
Inputs may be any that keep to these rules, and one draw needn't show every extreme that they name: `tile_ids`: for each crop and device the slots first hold distinct tiles of that device's region, numbered row by row with 4 to a row, then -1; each device lists exactly 2 tiles, so no slot holds -1.
All inputs are finite; a program needn't handle non-finite values.
Results may differ from a plain program's by a relative error of at most 0.027.
Values may be sent and summed in bfloat16 or wider, within the bound.
No kernel may reach another device: no remote copies, remote signals or barrier semaphores. Data moves between devices by JAX's collectives and lax.ppermute only.
A program may use at most 64 MiB of HBM per device.

v0:
```python
import jax
import jax.numpy as jnp
from jax import lax
from jax.sharding import PartitionSpec as P

D = 512
HEADS = 8
HD = 32
INNER = 256
TILE = 8
WIN = 7
HALO = 3
REG = 4
SIDE = 32
CAP = 2
ROWS = 128


def padded_2(array, sides, width):
    for axis, dim in sides:
        size, length = (lax.axis_size(axis), array.shape[dim])
        up = [(i, (i + 1) % size) for i in range(size - 1)]
        down = [(j, i) for i, j in up]
        last = lax.slice_in_dim(array, length - width, length, axis=dim)
        first = lax.slice_in_dim(array, 0, width, axis=dim)
        before = lax.ppermute(last, axis, up)
        after = lax.ppermute(first, axis, down)
        array = jnp.concatenate([before, array, after], axis=dim)
    return array


def window_tables():
    win_side = TILE + 2 * HALO
    query_cells = jnp.arange(TILE * TILE, dtype=jnp.int32)
    window_cells = jnp.arange(win_side * win_side, dtype=jnp.int32)
    row_step = (window_cells // win_side)[None, :] - HALO - (query_cells // TILE)[:, None]
    col_step = (window_cells % win_side)[None, :] - HALO - (query_cells % TILE)[:, None]
    inside = (jnp.abs(row_step) <= HALO) & (jnp.abs(col_step) <= HALO)
    offset = (row_step + HALO) * WIN + col_step + HALO
    onehot = (
        (offset[None, :, :] == jnp.arange(WIN * WIN, dtype=jnp.int32)[:, None, None])
        & inside[None, :, :]
    ).astype(jnp.float32)
    return (inside, onehot)


def softmax_scores(queries, key_rows, bias_table, allowed):
    scores = (
        jnp.einsum("nqhd,nkhd->nhqk", queries, key_rows, preferred_element_type=jnp.float32)
        * HD ** (-0.5)
        + bias_table[None]
    )
    scores = jnp.where(allowed, scores, -jnp.inf)
    row_max = jnp.max(scores, axis=-1, keepdims=True)
    exponent = jnp.exp(scores - row_max)
    return exponent / jnp.sum(exponent, axis=-1, keepdims=True)


def shards(tokens, tile_ids, w_qkv, w_out, norm_gain, rel_bias, update_grad):
    grid_high = lax.axis_size("gy")
    grid_wide = lax.axis_size("gx")
    my_row = lax.axis_index("gy")
    my_col = lax.axis_index("gx")
    win_side = TILE + 2 * HALO
    win_cells = win_side * win_side
    padded = SIDE + 2 * HALO
    block_slots = CAP
    block_count = CAP // block_slots
    inside, onehot = window_tables()
    bias_table = jnp.einsum("ho,oqk->hqk", rel_bias, onehot, precision=lax.Precision.HIGHEST)
    w_qkv_all, w_out_all = (
        lax.all_gather(w_qkv, "dp", axis=0, tiled=True),
        lax.all_gather(w_out, "dp", axis=0, tiled=True),
    )
    features = tokens.reshape(ROWS, D).astype(jnp.float32)
    inv_rms = lax.rsqrt(jnp.mean(features * features, axis=-1, keepdims=True) + 1e-06)
    normed = (features * inv_rms * norm_gain).astype(jnp.bfloat16)
    qkv_rows = jnp.dot(normed, w_qkv_all, preferred_element_type=jnp.float32).astype(jnp.bfloat16)
    crop_tiles = tile_ids.reshape(grid_high, grid_wide, CAP)
    slot_tiles = crop_tiles[my_row, my_col]
    is_active = slot_tiles >= 0
    tile_index = jnp.where(is_active, slot_tiles, 0)
    spare_local = REG * REG
    kv_tiles = qkv_rows[:, INNER:].reshape(CAP, TILE * TILE, 2 * INNER)
    tile_grid = (
        jnp.zeros((spare_local + 1, TILE * TILE, 2 * INNER), jnp.bfloat16)
        .at[jnp.where(is_active, slot_tiles, spare_local)]
        .set(kv_tiles)[:spare_local]
    )
    kv_region = (
        tile_grid.reshape(REG, REG, TILE, TILE, 2 * INNER)
        .transpose(0, 2, 1, 3, 4)
        .reshape(SIDE, SIDE, 2 * INNER)
    )
    kv_padded = padded_2(kv_region, (("gy", 0), ("gx", 1)), HALO)
    spare_tile = grid_high * REG * grid_wide * REG
    row_of_dev = jnp.arange(grid_high, dtype=jnp.int32)[:, None, None]
    col_of_dev = jnp.arange(grid_wide, dtype=jnp.int32)[None, :, None]
    flat_tiles = jnp.where(
        crop_tiles >= 0,
        (row_of_dev * REG + crop_tiles // REG) * (grid_wide * REG)
        + col_of_dev * REG
        + crop_tiles % REG,
        spare_tile,
    )
    crop_active = (
        jnp.zeros((spare_tile + 1,), jnp.float32)
        .at[flat_tiles.reshape(-1)]
        .set(1.0)[:spare_tile]
        .reshape(grid_high * REG, grid_wide * REG)
    )
    crop_active = jnp.pad(crop_active, 1)
    nearby = lax.dynamic_slice(crop_active, (my_row * REG, my_col * REG), (REG + 2, REG + 2))
    near_cells = jnp.repeat(jnp.repeat(nearby, TILE, axis=0), TILE, axis=1)
    key_active = (
        near_cells[TILE - HALO : TILE - HALO + padded, TILE - HALO : TILE - HALO + padded] > 0.5
    )
    start_rows = tile_index // REG * TILE
    start_cols = tile_index % REG * TILE
    zero_index = jnp.zeros((), jnp.int32)
    kv_windows = jax.vmap(
        lambda first_row, first_col: lax.dynamic_slice(
            kv_padded, (first_row, first_col, zero_index), (win_side, win_side, 2 * INNER)
        )
    )(start_rows, start_cols).reshape(CAP, win_cells, 2 * INNER)
    key_windows = jax.vmap(
        lambda first_row, first_col: lax.dynamic_slice(
            key_active, (first_row, first_col), (win_side, win_side)
        )
    )(start_rows, start_cols).reshape(CAP, win_cells)
    queries = qkv_rows[:, :INNER].reshape(block_count, block_slots, TILE * TILE, HEADS, HD)
    key_rows = kv_windows[:, :, :INNER].reshape(block_count, block_slots, win_cells, HEADS, HD)
    values = kv_windows[:, :, INNER:].reshape(block_count, block_slots, win_cells, HEADS, HD)
    allowed = (
        inside[None, None] & (key_windows[:, None, None, :] | ~is_active[:, None, None, None])
    ).reshape(block_count, block_slots, 1, TILE * TILE, win_cells)
    live = is_active.astype(jnp.float32).reshape(block_count, block_slots)

    def block_forward(block_items):
        query_block, key_block, value_block, allow_block, live_block = block_items
        attn_probs = softmax_scores(query_block, key_block, bias_table, allow_block)
        probs_bf = attn_probs.astype(jnp.bfloat16)
        attended = jnp.einsum(
            "nhqk,nkhd->nqhd", probs_bf, value_block, preferred_element_type=jnp.float32
        )
        return (attended * live_block[:, None, None, None]).astype(jnp.bfloat16)

    attended = lax.map(block_forward, (queries, key_rows, values, allowed, live)).reshape(
        ROWS, INNER
    )
    update = jnp.dot(attended, w_out_all, preferred_element_type=jnp.float32).astype(jnp.bfloat16)
    row_active = jnp.repeat(is_active, TILE * TILE)
    grad_rows = jnp.where(
        row_active[:, None], update_grad.reshape(ROWS, D), jnp.zeros((), jnp.bfloat16)
    )
    grad_attended = lax.dot_general(
        grad_rows, w_out_all, (((1,), (1,)), ((), ())), preferred_element_type=jnp.float32
    ).astype(jnp.bfloat16)
    grad_out_local = lax.dot_general(
        attended, grad_rows, (((0,), (0,)), ((), ())), preferred_element_type=jnp.float32
    )
    grad_heads = grad_attended.reshape(block_count, block_slots, TILE * TILE, HEADS, HD)

    def block_backward(block_items):
        query_block, key_block, value_block, allow_block, grad_block = block_items
        attn_probs = softmax_scores(query_block, key_block, bias_table, allow_block)
        probs_bf = attn_probs.astype(jnp.bfloat16)
        d_probs = jnp.einsum(
            "nqhd,nkhd->nhqk", grad_block, value_block, preferred_element_type=jnp.float32
        )
        row_delta = jnp.sum(attn_probs * d_probs, axis=-1, keepdims=True)
        d_scores = (attn_probs * (d_probs - row_delta)).astype(jnp.bfloat16)
        d_queries = jnp.einsum(
            "nhqk,nkhd->nqhd", d_scores, key_block, preferred_element_type=jnp.float32
        ) * HD ** (-0.5)
        d_keys = jnp.einsum(
            "nhqk,nqhd->nkhd", d_scores, query_block, preferred_element_type=jnp.float32
        ) * HD ** (-0.5)
        d_values = jnp.einsum(
            "nhqk,nqhd->nkhd", probs_bf, grad_block, preferred_element_type=jnp.float32
        )
        slot_part = d_keys.shape[0]
        d_kv = jnp.concatenate(
            [
                d_keys.reshape(slot_part, win_cells, INNER),
                d_values.reshape(slot_part, win_cells, INNER),
            ],
            axis=-1,
        )
        return (
            d_queries.reshape(slot_part, TILE * TILE, INNER),
            d_kv,
            jnp.sum(d_scores, axis=0, dtype=jnp.float32),
        )

    d_queries, d_kv_windows, bias_parts = lax.map(
        block_backward, (queries, key_rows, values, allowed, grad_heads)
    )
    grad_bias_sum = jnp.sum(bias_parts, axis=0)
    cell_index = jnp.arange(win_cells, dtype=jnp.int32)
    targets = (
        (start_rows[:, None] + cell_index[None, :] // win_side) * padded
        + start_cols[:, None]
        + cell_index[None, :] % win_side
    )
    grad_padded = (
        jnp.zeros((padded * padded, 2 * INNER), jnp.float32)
        .at[targets.reshape(-1)]
        .add(d_kv_windows.reshape(CAP * win_cells, 2 * INNER))
        .reshape(padded, padded, 2 * INNER)
    )
    returned = padded_2(grad_padded.astype(jnp.bfloat16), (("gy", 0), ("gx", 1)), HALO).astype(
        grad_padded.dtype
    )
    start_in = 2 * HALO
    start_far = padded + HALO
    own_grad = grad_padded[HALO : HALO + SIDE, HALO : HALO + SIDE]
    own_grad = own_grad.at[:HALO, :].add(returned[:HALO, start_in : start_in + SIDE])
    own_grad = own_grad.at[SIDE - HALO :, :].add(returned[start_far:, start_in : start_in + SIDE])
    own_grad = own_grad.at[:, :HALO].add(returned[start_in : start_in + SIDE, :HALO])
    own_grad = own_grad.at[:, SIDE - HALO :].add(returned[start_in : start_in + SIDE, start_far:])
    own_grad = own_grad.at[:HALO, :HALO].add(returned[:HALO, :HALO])
    own_grad = own_grad.at[:HALO, SIDE - HALO :].add(returned[:HALO, start_far:])
    own_grad = own_grad.at[SIDE - HALO :, :HALO].add(returned[start_far:, :HALO])
    own_grad = own_grad.at[SIDE - HALO :, SIDE - HALO :].add(returned[start_far:, start_far:])
    grad_tiles = (
        own_grad.reshape(REG, TILE, REG, TILE, 2 * INNER)
        .transpose(0, 2, 1, 3, 4)
        .reshape(REG * REG, TILE * TILE, 2 * INNER)
    )
    grad_slots = jnp.where(is_active[:, None, None], grad_tiles[tile_index], 0.0)
    grad_qkv_rows = jnp.concatenate(
        [d_queries.reshape(ROWS, INNER), grad_slots.reshape(ROWS, 2 * INNER)], axis=-1
    ).astype(jnp.bfloat16)
    grad_qkv_local = lax.dot_general(
        normed, grad_qkv_rows, (((0,), (0,)), ((), ())), preferred_element_type=jnp.float32
    )
    grad_normed = lax.dot_general(
        grad_qkv_rows, w_qkv_all, (((1,), (1,)), ((), ())), preferred_element_type=jnp.float32
    )
    scaled_grad = grad_normed * norm_gain
    gain_local = jnp.sum(grad_normed * features * inv_rms, axis=0)
    grad_tokens = (
        inv_rms * scaled_grad
        - features * inv_rms**3 * jnp.mean(scaled_grad * features, axis=-1, keepdims=True)
    ).astype(jnp.bfloat16)
    bias_local = jnp.einsum("hqk,oqk->ho", grad_bias_sum, onehot, precision=lax.Precision.HIGHEST)
    grad_gain, grad_bias = lax.psum((gain_local, bias_local), ("gy", "gx", "dp"))
    qkv_whole, out_whole = (
        lax.psum(grad_qkv_local.astype(jnp.bfloat16), ("gy", "gx")).astype(jnp.float32),
        lax.psum(grad_out_local.astype(jnp.bfloat16), ("gy", "gx")).astype(jnp.float32),
    )
    grad_qkv, grad_out = (
        lax.psum_scatter(
            qkv_whole.astype(jnp.bfloat16), "dp", scatter_dimension=0, tiled=True
        ).astype(jnp.float32),
        lax.psum_scatter(
            out_whole.astype(jnp.bfloat16), "dp", scatter_dimension=0, tiled=True
        ).astype(jnp.float32),
    )
    return (
        update.reshape(tokens.shape),
        grad_tokens.reshape(tokens.shape),
        grad_qkv,
        grad_out,
        grad_gain,
        grad_bias,
    )


def solution(mesh):
    return jax.shard_map(
        shards,
        mesh=mesh,
        in_specs=(
            P("dp", "gy", "gx", None, None),
            P("dp", None, None, None),
            P("dp", None),
            P("dp", None),
            P(),
            P(),
            P("dp", "gy", "gx", None, None),
        ),
        out_specs=(
            P("dp", "gy", "gx", None, None),
            P("dp", "gy", "gx", None, None),
            P("dp", None),
            P("dp", None),
            P(),
            P(),
        ),
        check_vma=False,
    )
```

profile of v0, /device:TPU:1, one launch (start us, length us, event | category | flops | bytes accessed | tf_op | source)
XLA Modules:
  0.0 688.9 jit_solution(10179969984633198570)
XLA Ops:
  7.2 1.0 fusion.29
  8.8 0.9 dynamic-slice_reduce_fusion
  9.7 40.1 %all_gather.6 = bf16[512,768]{1,0:T(8,128)(2,1)S(1)} all-gather(bf16[16,768]{1,0:T(8,128)(2,1)} %param.25), channel_id=1, replica_groups=mesh['gy'=4,'gx'=4,'dp'=32] {'dp'}, dimensions={0}, use_global_device_ids=true | all-gather | bytes 811008 | tf_op jit(solution)/shard_map/all_gather | solution.py:72
  49.8 1.3 convolution_convert_fusion.2
  52.2 22.8 %collective-permute-start = (bf16[3,32,512]{2,1,0:T(8,128)(2,1)S(1)}, bf16[3,32,512]{2,1,0:T(8,128)(2,1)S(1)}, u32[]{:S(2)}, u32[]{:S(2)}) collective-permute-start(bf16[3,32,512]{2,1,0:T(8,128)(2,1)S(1)} %get-tuple-element.240), channel_id=1, source_target_pairs={{0,128},{128,256},{256,384},{1,129},{129,257},{257,385},{2,130},{1... | collective-permute-start | bytes 294920 | tf_op jit(solution)/shard_map/ppermute | solution.py:26
  75.0 1.9 collective-permute-start.1
  79.4 0.7 scatter_custom_fusion.1
  80.6 4.2 while.21
  81.2 1.4 dynamic-slice.90
  83.3 1.4 dynamic-slice.90
  84.9 35.8 %all_gather.7 = bf16[256,512]{1,0:T(8,128)(2,1)S(1)} all-gather(bf16[8,512]{1,0:T(8,128)(2,1)S(1)} %copy-done.20), channel_id=1, replica_groups=mesh['gy'=4,'gx'=4,'dp'=32] {'dp'}, dimensions={0}, use_global_device_ids=true | all-gather | bytes 270336 | tf_op jit(solution)/shard_map/all_gather | solution.py:73
  120.8 0.7 broadcast_and_fusion
  121.4 1.4 fusion.16
  123.3 2.8 collective-permute-start.2
  126.1 1.5 collective-permute-start.3
  127.8 0.8 squeeze.42
  129.0 0.7 and_reduce_fusion
  129.7 0.7 copy-done.12
  130.4 1.8 collective-permute-done.3
  132.1 1.9 pad_maximum_fusion
  134.0 5.5 while.20
  134.7 2.1 bitcast_dynamic-update-slice_fusion.4
  137.4 2.1 bitcast_dynamic-update-slice_fusion.4
  139.5 1.5 copy.67
  142.3 0.8 convolution_bitcast_fusion
  144.1 0.8 fusion.23
  145.1 0.7 reshape.1052
  146.3 1.2 convert_reduce_fusion
  148.6 1.2 copy.85
  149.9 4.2 scatter_custom_fusion.2
  154.0 2.0 reshape.1056
  156.0 2.1 convert_element_type.82
  158.1 21.3 %collective-permute-start.4 = (bf16[3,38,512]{2,1,0:T(8,128)(2,1)S(1)}, bf16[3,38,512]{2,1,0:T(8,128)(2,1)S(1)}, u32[]{:S(2)}, u32[]{:S(2)}) collective-permute-start(bf16[3,38,512]{2,1,0:T(8,128)(2,1)S(1)} %get-tuple-element.236), channel_id=1, source_target_pairs={{0,128},{128,256},{256,384},{1,129},{129,257},{257,385},{2,130},{1... | collective-permute-start | bytes 350216 | tf_op jit(solution)/shard_map/ppermute | solution.py:26
  179.5 1.9 collective-permute-start.5
  181.5 1.0 convolution_convert_fusion.1
  182.4 3.5 slice.355
  186.0 3.7 collective-permute-done.5
  189.7 0.8 pad_maximum_fusion.5
  190.5 4.3 collective-permute-start.6
  194.9 1.5 collective-permute-start.7
  197.6 4.5 collective-permute-done.7
  202.0 1.7 fusion.42
  203.7 1.7 fusion.41
  205.4 1.2 convert_add_fusion.1
  206.6 3.8 scatter-add.39
  210.3 1.2 convert_add_fusion
  211.6 3.2 scatter-add.40
  214.7 0.8 convert_add_fusion.5
  215.6 1.5 scatter-add.41
  217.1 2.7 add_select_fusion
  219.8 2.8 scatter-add.44
  222.5 0.8 convert_add_fusion.4
  223.4 1.5 scatter-add.54
  224.9 0.8 slice_add_fusion
  225.7 1.5 scatter-add.55
  227.2 1.8 copy.86
  229.7 1.3 convolution_convert_fusion
  231.1 0.9 fusion.24
  232.0 2.1 fusion.25
  234.6 96.2 %all-reduce.1 = (f32[512]{0:T(512)}, f32[8,49]{1,0:T(8,128)}) all-reduce(f32[512]{0:T(512)S(1)} %get-tuple-element.204, f32[8,49]{1,0:T(8,128)S(1)} %fusion.25), channel_id=1, replica_groups=mesh['gy'=4,'gx'=4,'dp'=32] {'gy','gx','dp'}, use_global_device_ids=true, to_apply=%region_14.15 | all-reduce | flops 904 | bytes 7232 | tf_op jit(solution)/shard_map/psum | solution.py:248
  330.8 0.8 fusion.43
  331.6 66.2 %reduce-scatter.5.cloned.1.call-done = bf16[8,512]{1,0:T(8,128)(2,1)} async-done(((bf16[256,512]{1,0:T(8,128)(2,1)}), bf16[8,512]{1,0:T(8,128)(2,1)}) %reduce-scatter.5.cloned.1.call-update) | async-done | bytes 8208 | tf_op jit(solution)/shard_map/reduce_scatter | solution.py:257
  397.8 223.2 %reduce-scatter.3.cloned.1.call-done = bf16[16,768]{1,0:T(8,128)(2,1)} async-done(((bf16[512,768]{1,0:T(8,128)(2,1)}), bf16[16,768]{1,0:T(8,128)(2,1)}) %reduce-scatter.3.cloned.1.call-update) | async-done | bytes 24592 | tf_op jit(solution)/shard_map/reduce_scatter | solution.py:254
  621.0 59.8 %all-reduce.2 = (bf16[16,768]{1,0:T(8,128)(2,1)S(1)}, bf16[8,512]{1,0:T(8,128)(2,1)S(1)}) all-reduce(bf16[16,768]{1,0:T(8,128)(2,1)} %reduce-scatter.3.cloned.1.call-done, bf16[8,512]{1,0:T(8,128)(2,1)} %reduce-scatter.5.cloned.1.call-done), channel_id=1, replica_groups=mesh['gy'=4,'gx'=4,'dp'=32] {'gy','gx'}, use_global_device_ids=true, to_apply=%region_9.10 | all-reduce | flops 16384 | bytes 65536 | tf_op jit(solution)/shard_map/psum | solution.py:250
  (154 shorter events, 16.0 us)
Async XLA Ops:
  7.2 114.3 %copy-start = (f32[8,49]{1,0:T(8,128)S(1)}, f32[8,49]{1,0:T(8,128)}, u32[]{:S(2)}) copy-start(f32[8,49]{1,0:T(8,128)} %param.28) | copy-start | bytes 4708
  7.2 390.6 %reduce-scatter.5.cloned.1.call-start = ((), (), s32[]{:S(2)}) async-start(), calls=%async_computation.3 | async-start | bytes 270336 | tf_op jit(solution)/shard_map/reduce_scatter | solution.py:257
  49.8 1.4 copy-start.1
  51.9 25.6 %copy-start.21 = (s32[1,4,4,2]{2,3,1,0:T(2,128)S(1)}, s32[1,4,4,2]{2,3,1,0:T(2,128)}, u32[]{:S(2)}) copy-start(s32[1,4,4,2]{2,3,1,0:T(2,128)} %param.24) | copy-start | bytes 388
  51.9 33.0 %copy-start.20 = (bf16[8,512]{1,0:T(8,128)(2,1)S(1)}, bf16[8,512]{1,0:T(8,128)(2,1)}, u32[]{:S(2)}) copy-start(bf16[8,512]{1,0:T(8,128)(2,1)} %param.26) | copy-start | bytes 24580
  52.0 70.9 %copy-start.15 = (bf16[1,1,1,128,512]{4,3,2,1,0:T(8,128)(2,1)S(1)}, bf16[1,1,1,128,512]{4,3,2,1,0:T(8,128)(2,1)}, u32[]{:S(2)}) copy-start(bf16[1,1,1,128,512]{4,3,2,1,0:T(8,128)(2,1)} %param.29) | copy-start | bytes 393220
  52.2 71.0 %collective-permute-start = (bf16[3,32,512]{2,1,0:T(8,128)(2,1)S(1)}, bf16[3,32,512]{2,1,0:T(8,128)(2,1)S(1)}, u32[]{:S(2)}, u32[]{:S(2)}) collective-permute-start(bf16[3,32,512]{2,1,0:T(8,128)(2,1)S(1)} %get-tuple-element.240), channel_id=1, source_target_pairs={{0,128},{128,256},{256,384},{1,129},{129,257},{257,385},{2,130},{1... | collective-permute-start | bytes 294920 | tf_op jit(solution)/shard_map/ppermute | solution.py:26
  75.0 48.2 %collective-permute-start.1 = (bf16[3,32,512]{2,1,0:T(8,128)(2,1)S(1)}, bf16[3,32,512]{2,1,0:T(8,128)(2,1)S(1)}, u32[]{:S(2)}, u32[]{:S(2)}) collective-permute-start(bf16[3,32,512]{2,1,0:T(8,128)(2,1)S(1)} %get-tuple-element.241), channel_id=1, source_target_pairs={{128,0},{256,128},{384,256},{129,1},{257,129},{385,257},{130,2},{2... | collective-permute-start | bytes 294920 | tf_op jit(solution)/shard_map/ppermute | solution.py:27
  77.8 45.5 %copy-start.17 = (s32[64,196]{1,0:T(8,128)}, s32[64,196]{1,0:T(8,128)S(1)}, u32[]{:S(2)}) copy-start(s32[64,196]{1,0:T(8,128)S(1)} %fusion.57) | copy-start | bytes 150532
  78.6 44.6 %copy-start.22 = (pred[128]{0:T(512)(128)(4,1)}, pred[128]{0:T(512)(128)(4,1)S(1)}, u32[]{:S(2)}) copy-start(pred[128]{0:T(512)(128)(4,1)S(1)} %broadcast_in_dim.152) | copy-start | bytes 388
  120.7 2.2 copy-start.8
  122.9 6.1 copy-start.25
  123.3 6.4 collective-permute-start.2
  126.1 6.1 collective-permute-start.3
  129.0 15.1 %copy-start.6 = (bf16[2,64,8,32]{1,0,3,2:T(2,128)(2,1)}, bf16[2,64,8,32]{1,0,3,2:T(2,128)(2,1)S(1)}, u32[]{:S(2)}) copy-start(bf16[2,64,8,32]{1,0,3,2:T(2,128)(2,1)S(1)} %squeeze.40) | copy-start | bytes 196612
  129.7 0.7 copy-start.12
  139.5 2.2 copy-start.13
  139.5 2.8 copy-start.14
  141.5 2.6 copy-start.3
  143.1 0.9 copy-start.26
  146.3 1.2 copy-start.7
  156.0 25.4 %copy-start.10 = (bf16[128,256]{0,1:T(8,128)(2,1)S(1)}, bf16[128,256]{0,1:T(8,128)(2,1)}, u32[]{:S(2)}) copy-start(bf16[128,256]{0,1:T(8,128)(2,1)} %reshape.1052) | copy-start | bytes 196612
  156.0 25.4 %copy-start.16 = (bf16[1,1,1,128,512]{4,3,2,1,0:T(8,128)(2,1)S(1)}, bf16[1,1,1,128,512]{4,3,2,1,0:T(8,128)(2,1)}, u32[]{:S(2)}) copy-start(bf16[1,1,1,128,512]{4,3,2,1,0:T(8,128)(2,1)} %param.29) | copy-start | bytes 393220
  156.0 25.5 %copy-start.23 = (pred[128]{0:T(512)(128)(4,1)S(1)}, pred[128]{0:T(512)(128)(4,1)}, u32[]{:S(2)}) copy-start(pred[128]{0:T(512)(128)(4,1)} %copy-done.22) | copy-start | bytes 388
  158.1 27.8 %collective-permute-start.4 = (bf16[3,38,512]{2,1,0:T(8,128)(2,1)S(1)}, bf16[3,38,512]{2,1,0:T(8,128)(2,1)S(1)}, u32[]{:S(2)}, u32[]{:S(2)}) collective-permute-start(bf16[3,38,512]{2,1,0:T(8,128)(2,1)S(1)} %get-tuple-element.236), channel_id=1, source_target_pairs={{0,128},{128,256},{256,384},{1,129},{129,257},{257,385},{2,130},{1... | collective-permute-start | bytes 350216 | tf_op jit(solution)/shard_map/ppermute | solution.py:26
  179.5 10.2 %collective-permute-start.5 = (bf16[3,38,512]{2,1,0:T(8,128)(2,1)S(1)}, bf16[3,38,512]{2,1,0:T(8,128)(2,1)S(1)}, u32[]{:S(2)}, u32[]{:S(2)}) collective-permute-start(bf16[3,38,512]{2,1,0:T(8,128)(2,1)S(1)} %get-tuple-element.237), channel_id=1, source_target_pairs={{128,0},{256,128},{384,256},{129,1},{257,129},{385,257},{130,2},{2... | collective-permute-start | bytes 350216 | tf_op jit(solution)/shard_map/ppermute | solution.py:27
  185.9 10.5 %copy-start.4 = (bf16[2,196,256]{1,2,0:T(8,128)(2,1)S(1)}, bf16[2,196,256]{1,2,0:T(8,128)(2,1)}, u32[]{:S(2)}) copy-start(bf16[2,196,256]{1,2,0:T(8,128)(2,1)} %copy-done.3) | copy-start | bytes 602116
  185.9 435.0 %reduce-scatter.3.cloned.1.call-start = ((), (), s32[]{:S(2)}) async-start(), calls=%async_computation.2 | async-start | bytes 811008 | tf_op jit(solution)/shard_map/reduce_scatter | solution.py:254
  190.5 7.0 %collective-permute-start.6 = (bf16[44,3,512]{2,1,0:T(4,128)(2,1)}, bf16[44,3,512]{2,1,0:T(4,128)(2,1)S(1)}, u32[]{:S(2)}, u32[]{:S(2)}) collective-permute-start(bf16[44,3,512]{2,1,0:T(4,128)(2,1)} %get-tuple-element.234), channel_id=1, source_target_pairs={{0,32},{32,64},{64,96},{1,33},{33,65},{65,97},{2,34},{34,66},{66,9... | collective-permute-start | bytes 405512 | tf_op jit(solution)/shard_map/ppermute | solution.py:26
  194.9 7.2 %collective-permute-start.7 = (bf16[44,3,512]{2,1,0:T(4,128)(2,1)S(1)}, bf16[44,3,512]{2,1,0:T(4,128)(2,1)S(1)}, u32[]{:S(2)}, u32[]{:S(2)}) collective-permute-start(bf16[44,3,512]{2,1,0:T(4,128)(2,1)S(1)} %get-tuple-element.235), channel_id=1, source_target_pairs={{32,0},{64,32},{96,64},{33,1},{65,33},{97,65},{34,2},{66,34},{98,6... | collective-permute-start | bytes 405512 | tf_op jit(solution)/shard_map/ppermute | solution.py:27
  225.7 4.0 copy-start.5
  225.7 4.0 copy-start.19
  227.2 3.9 copy-start.9
  229.0 3.0 copy-start.11
  229.0 3.0 copy-start.18
  229.7 4.4 copy-start.2
  231.1 99.7 %copy-start.24 = (f32[128]{0:T(128)S(1)}, f32[128]{0:T(128)}, u32[]{:S(2)}) copy-start(f32[128]{0:T(128)} %get-tuple-element.244) | copy-start | bytes 1540
Sparse Core Ops, SparseCore 0:
  186.1 211.6 reduce-scatter.4
  402.8 218.1 reduce-scatter.2
where the time goes:
time: 690 us; the launch traced here: 689 us
  waiting for transfers between devices  300 us (43%)
  blocking collectives  232 us (34%)
  starting transfers between devices  58.1 us (8%)
  local copies, waits for them, and re-layouts  44.6 us (6%)
  other arithmetic  27.4 us (4%)
  between operations  14.9 us (2%)
  matrix products  12.1 us (2%)
    reduce_scatter x1, waiting for transfers between devices, shards(): lax.psum_scatter(qkv_whole.astype(jnp.bfloat16), 'dp', scatter_dimension=...  223 us
    psum x1, blocking collectives, shards(): lax.psum((gain_local, bias_local), ('gy', 'gx', 'dp'))  96.2 us
    reduce_scatter x1, waiting for transfers between devices, shards(): lax.psum_scatter(out_whole.astype(jnp.bfloat16), 'dp', scatter_dimension=...  66.2 us
    psum x1, blocking collectives, shards(): lax.psum(grad_qkv_local.astype(jnp.bfloat16), ('gy', 'gx'))  59.8 us
    ppermute x4, starting transfers between devices, padded_2(): before = lax.ppermute(last, axis, up)  51.2 us
    all_gather x1, blocking collectives, shards(): lax.all_gather(w_qkv, 'dp', axis=0, tiled=True)  40.1 us
    all_gather x1, blocking collectives, shards(): lax.all_gather(w_out, 'dp', axis=0, tiled=True)  35.8 us
  transfers between devices with their start and end apart: 10, of which 6 were waited for; matrix products, arithmetic and copies ran while one was open for 7% of the time, Pallas kernels for 0%

commit v1 on v0

--- a/solution.py
+++ b/solution.py
@@ -2,6 +2,7 @@
 import jax.numpy as jnp
 from jax import lax
 from jax.sharding import PartitionSpec as P
+from jax.lax import all_to_all, axis_size
 
 D = 512
 HEADS = 8
@@ -70,7 +71,15 @@
     bias_table = jnp.einsum("ho,oqk->hqk", rel_bias, onehot, precision=lax.Precision.HIGHEST)
     w_qkv_all, w_out_all = (
         lax.all_gather(w_qkv, "dp", axis=0, tiled=True),
-        lax.all_gather(w_out, "dp", axis=0, tiled=True),
+        jnp.concatenate(
+            all_to_all(
+                jnp.stack([w_out] * axis_size("dp"), axis=0),
+                axis_name="dp",
+                split_axis=0,
+                concat_axis=0,
+            ),
+            0,
+        ),
     )
     features = tokens.reshape(ROWS, D).astype(jnp.float32)
     inv_rms = lax.rsqrt(jnp.mean(features * features, axis=-1, keepdims=True) + 1e-06)

time: 690 us -> 652 us (0.945)
  blocking collectives: 232 us -> 195 us
    all_gather x1 -> x0, blocking collectives: 35.8 us -> none  [shards(): lax.all_gather(w_out, 'dp', axis=0, tiled=True)]
    ppermute x4, starting transfers between devices: 51.2 us -> 39.2 us  [padded_2(): before = lax.ppermute(last, axis, up)]
    all_to_all x0 -> x1, starting transfers between devices: none -> 10.5 us  [shards(): all_to_all(jnp.stack([w_out] * axis_size('dp'), axis=0), axis_name='dp',...]
  transfers between devices with their start and end apart: 10 -> 11, of which waited for: 6 -> 6; matrix products, arithmetic and copies ran while one was open for 7% -> 11% of each run, Pallas kernels for 0% -> 0%
where the time goes in v1:
time: 652 us; the launch traced here: 650 us
  waiting for transfers between devices  296 us (45%)
  blocking collectives  195 us (30%)
  starting transfers between devices  56.6 us (9%)
  local copies, waits for them, and re-layouts  47.6 us (7%)
  other arithmetic  27.5 us (4%)
  between operations  14.9 us (2%)
  matrix products  12.1 us (2%)
    reduce_scatter x1, waiting for transfers between devices, shards(): lax.psum_scatter(qkv_whole.astype(jnp.bfloat16), 'dp', scatter_dimension=...  223 us
    psum x1, blocking collectives, shards(): lax.psum((gain_local, bias_local), ('gy', 'gx', 'dp'))  96.5 us
    reduce_scatter x1, waiting for transfers between devices, shards(): lax.psum_scatter(out_whole.astype(jnp.bfloat16), 'dp', scatter_dimension=...  63.4 us
    psum x1, blocking collectives, shards(): lax.psum(grad_qkv_local.astype(jnp.bfloat16), ('gy', 'gx'))  59.8 us
    ppermute x4, starting transfers between devices, padded_2(): before = lax.ppermute(last, axis, up)  39.2 us
    all_gather x1, blocking collectives, shards(): lax.all_gather(w_qkv, 'dp', axis=0, tiled=True)  39.1 us
  transfers between devices with their start and end apart: 11, of which 6 were waited for; matrix products, arithmetic and copies ran while one was open for 11% of the time, Pallas kernels for 0%

profile of v1, /device:TPU:1, one launch (start us, length us, event | category | flops | bytes accessed | tf_op | source)
XLA Modules:
  0.0 650.0 jit_solution(3756850234880267005)
XLA Ops:
  7.2 1.4 stack.2
  8.6 10.5 %all-to-all-start = ((bf16[32,8,512]{2,1,0:T(8,128)(2,1)}), bf16[32,8,512]{2,1,0:T(8,128)(2,1)S(1)}, u32[]{:S(2)}, u32[]{:S(2)}) async-start(bf16[32,8,512]{2,1,0:T(8,128)(2,1)} %stack.2), calls=%async_computation | async-start | bytes 524288 | tf_op jit(solution)/shard_map/all_to_all | solution.py:75
  19.2 1.0 fusion.29
  20.7 0.9 dynamic-slice_reduce_fusion
  21.6 39.1 %all_gather.3 = bf16[512,768]{1,0:T(8,128)(2,1)S(1)} all-gather(bf16[16,768]{1,0:T(8,128)(2,1)} %param.25), channel_id=1, replica_groups=mesh['gy'=4,'gx'=4,'dp'=32] {'dp'}, dimensions={0}, use_global_device_ids=true | all-gather | bytes 811008 | tf_op jit(solution)/shard_map/all_gather | solution.py:73
  60.6 1.3 convolution_convert_fusion.2
  63.0 22.8 %collective-permute-start = (bf16[3,32,512]{2,1,0:T(8,128)(2,1)S(1)}, bf16[3,32,512]{2,1,0:T(8,128)(2,1)S(1)}, u32[]{:S(2)}, u32[]{:S(2)}) collective-permute-start(bf16[3,32,512]{2,1,0:T(8,128)(2,1)S(1)} %get-tuple-element.240), channel_id=1, source_target_pairs={{0,128},{128,256},{256,384},{1,129},{129,257},{257,385},{2,130},{1... | collective-permute-start | bytes 294920 | tf_op jit(solution)/shard_map/ppermute | solution.py:27
  85.8 1.9 collective-permute-start.1
  90.1 0.7 scatter_custom_fusion.1
  91.3 4.2 while.21
  91.9 1.4 dynamic-slice.90
  94.0 1.4 dynamic-slice.90
  96.3 1.4 fusion.16
  98.0 3.1 collective-permute-start.2
  101.1 1.5 collective-permute-start.3
  104.4 0.7 and_reduce_fusion
  105.8 1.3 collective-permute-done.3
  107.1 2.0 pad_maximum_fusion
  109.1 6.8 %while.20 = (s32[]{:T(128)}, bf16[38,38,512]{2,1,0:T(8,128)(2,1)S(1)}, s32[2,3]{1,0:T(2,128)}, bf16[2,14,14,512]{3,2,1,0:T(8,128)(2,1)}, s32[]{:T(128)}) while((s32[]{:T(128)}, bf16[38,38,512]{2,1,0:T(8,128)(2,1)S(1)}, s32[2,3]{1,0:T(2,128)}, bf16[2,14,14,512]{3,2,1,0:T(8,128)(2,1)}, s32[]{:T(128)}) %tuple.102), condition=%wide.while_cond.8, body=%wide.while_body.8.sunk | while | flops 2 | bytes 431221 | solution.py:131
  109.1 0.7 constant_dynamic-slice_fusion.4
  110.4 2.1 bitcast_dynamic-update-slice_fusion.4
  112.5 0.7 constant_dynamic-slice_fusion.4
  113.8 2.1 bitcast_dynamic-update-slice_fusion.4
  115.9 1.4 copy.67
  118.7 0.8 fusion.23
  119.7 0.7 reshape.1063
  121.0 0.8 convolution_bitcast_fusion
  123.2 1.2 convert_reduce_fusion
  125.5 1.2 copy.85
  126.7 4.2 scatter_custom_fusion.2
  130.9 2.0 reshape.1067
  132.9 2.1 convert_element_type.82
  135.0 9.0 %collective-permute-start.4 = (bf16[3,38,512]{2,1,0:T(8,128)(2,1)S(1)}, bf16[3,38,512]{2,1,0:T(8,128)(2,1)S(1)}, u32[]{:S(2)}, u32[]{:S(2)}) collective-permute-start(bf16[3,38,512]{2,1,0:T(8,128)(2,1)S(1)} %get-tuple-element.236), channel_id=1, source_target_pairs={{0,128},{128,256},{256,384},{1,129},{129,257},{257,385},{2,130},{1... | collective-permute-start | bytes 350216 | tf_op jit(solution)/shard_map/ppermute | solution.py:27
  144.0 1.9 collective-permute-start.5
  146.0 1.0 convolution_convert_fusion.1
  147.0 3.5 slice.355
  150.5 3.7 collective-permute-done.5
  154.2 0.8 pad_maximum_fusion.5
  155.0 4.3 collective-permute-start.6
  159.4 1.5 collective-permute-start.7
  162.1 3.7 collective-permute-done.7
  165.8 1.7 fusion.44
  167.5 1.6 fusion.43
  169.1 1.2 convert_add_fusion.1
  170.3 3.8 scatter-add.39
  174.1 1.2 convert_add_fusion
  175.4 3.2 scatter-add.40
  178.5 0.8 convert_add_fusion.5
  179.4 1.5 scatter-add.41
  180.8 2.7 add_select_fusion
  183.5 2.6 scatter-add.44
  186.1 0.8 convert_add_fusion.4
  186.9 1.5 scatter-add.54
  188.4 0.8 slice_add_fusion
  189.3 1.5 scatter-add.55
  190.8 1.8 copy.86
  193.3 1.4 convolution_convert_fusion
  194.7 0.9 fusion.24
  195.6 2.1 fusion.25
  198.2 96.5 %all-reduce.1 = (f32[512]{0:T(512)}, f32[8,49]{1,0:T(8,128)}) all-reduce(f32[512]{0:T(512)S(1)} %get-tuple-element.204, f32[8,49]{1,0:T(8,128)S(1)} %fusion.25), channel_id=1, replica_groups=mesh['gy'=4,'gx'=4,'dp'=32] {'gy','gx','dp'}, use_global_device_ids=true, to_apply=%region_14.15 | all-reduce | flops 904 | bytes 7232 | tf_op jit(solution)/shard_map/psum | solution.py:257
  294.7 0.8 fusion.45
  295.5 63.4 %reduce-scatter.5.cloned.1.call-done = bf16[8,512]{1,0:T(8,128)(2,1)} async-done(((bf16[256,512]{1,0:T(8,128)(2,1)}), bf16[8,512]{1,0:T(8,128)(2,1)}) %reduce-scatter.5.cloned.1.call-update) | async-done | bytes 8208 | tf_op jit(solution)/shard_map/reduce_scatter | solution.py:266
  358.9 223.3 %reduce-scatter.3.cloned.1.call-done = bf16[16,768]{1,0:T(8,128)(2,1)} async-done(((bf16[512,768]{1,0:T(8,128)(2,1)}), bf16[16,768]{1,0:T(8,128)(2,1)}) %reduce-scatter.3.cloned.1.call-update) | async-done | bytes 24592 | tf_op jit(solution)/shard_map/reduce_scatter | solution.py:263
  582.2 59.8 %all-reduce.2 = (bf16[16,768]{1,0:T(8,128)(2,1)S(1)}, bf16[8,512]{1,0:T(8,128)(2,1)S(1)}) all-reduce(bf16[16,768]{1,0:T(8,128)(2,1)} %reduce-scatter.3.cloned.1.call-done, bf16[8,512]{1,0:T(8,128)(2,1)} %reduce-scatter.5.cloned.1.call-done), channel_id=1, replica_groups=mesh['gy'=4,'gx'=4,'dp'=32] {'gy','gx'}, use_global_device_ids=true, to_apply=%region_9.10 | all-reduce | flops 16384 | bytes 65536 | tf_op jit(solution)/shard_map/psum | solution.py:259
  (156 shorter events, 18.5 us)
Async XLA Ops:
  7.2 89.2 %copy-start = (f32[8,49]{1,0:T(8,128)S(1)}, f32[8,49]{1,0:T(8,128)}, u32[]{:S(2)}) copy-start(f32[8,49]{1,0:T(8,128)} %param.28) | copy-start | bytes 4708
  8.6 111.9 %all-to-all-start = ((bf16[32,8,512]{2,1,0:T(8,128)(2,1)}), bf16[32,8,512]{2,1,0:T(8,128)(2,1)S(1)}, u32[]{:S(2)}, u32[]{:S(2)}) async-start(bf16[32,8,512]{2,1,0:T(8,128)(2,1)} %stack.2), calls=%async_computation | async-start | bytes 524288 | tf_op jit(solution)/shard_map/all_to_all | solution.py:75
  19.1 339.8 %reduce-scatter.5.cloned.1.call-start = ((), (), s32[]{:S(2)}) async-start(), calls=%async_computation.4 | async-start | bytes 270336 | tf_op jit(solution)/shard_map/reduce_scatter | solution.py:266
  60.6 1.4 copy-start.1
  62.7 25.7 %copy-start.21 = (s32[1,4,4,2]{2,3,1,0:T(2,128)S(1)}, s32[1,4,4,2]{2,3,1,0:T(2,128)}, u32[]{:S(2)}) copy-start(s32[1,4,4,2]{2,3,1,0:T(2,128)} %param.24) | copy-start | bytes 388
  63.0 34.8 %collective-permute-start = (bf16[3,32,512]{2,1,0:T(8,128)(2,1)S(1)}, bf16[3,32,512]{2,1,0:T(8,128)(2,1)S(1)}, u32[]{:S(2)}, u32[]{:S(2)}) collective-permute-start(bf16[3,32,512]{2,1,0:T(8,128)(2,1)S(1)} %get-tuple-element.240), channel_id=1, source_target_pairs={{0,128},{128,256},{256,384},{1,129},{129,257},{257,385},{2,130},{1... | collective-permute-start | bytes 294920 | tf_op jit(solution)/shard_map/ppermute | solution.py:27
  85.8 12.0 %collective-permute-start.1 = (bf16[3,32,512]{2,1,0:T(8,128)(2,1)S(1)}, bf16[3,32,512]{2,1,0:T(8,128)(2,1)S(1)}, u32[]{:S(2)}, u32[]{:S(2)}) collective-permute-start(bf16[3,32,512]{2,1,0:T(8,128)(2,1)S(1)} %get-tuple-element.241), channel_id=1, source_target_pairs={{128,0},{256,128},{384,256},{129,1},{257,129},{385,257},{130,2},{2... | collective-permute-start | bytes 294920 | tf_op jit(solution)/shard_map/ppermute | solution.py:28
  88.8 9.0 %copy-start.18 = (s32[64,196]{1,0:T(8,128)}, s32[64,196]{1,0:T(8,128)S(1)}, u32[]{:S(2)}) copy-start(s32[64,196]{1,0:T(8,128)S(1)} %fusion.57) | copy-start | bytes 150532
  96.3 8.1 %copy-start.25 = (s32[3]{0:T(128)S(1)}, s32[3]{0:T(128)}, u32[]{:S(2)}) copy-start(s32[3]{0:T(128)} %constant.428.clone.1) | copy-start | bytes 40
  97.8 7.4 %copy-start.12 = (bf16[3,32,512]{2,1,0:T(8,128)(2,1)}, bf16[3,32,512]{2,1,0:T(8,128)(2,1)S(1)}, u32[]{:S(2)}) copy-start(bf16[3,32,512]{2,1,0:T(8,128)(2,1)S(1)} %collective-permute-done) | copy-start | bytes 294916
  97.8 7.3 %copy-start.13 = (bf16[3,32,512]{2,1,0:T(8,128)(2,1)}, bf16[3,32,512]{2,1,0:T(8,128)(2,1)S(1)}, u32[]{:S(2)}) copy-start(bf16[3,32,512]{2,1,0:T(8,128)(2,1)S(1)} %collective-permute-done.1) | copy-start | bytes 294916
  98.0 7.2 %collective-permute-start.2 = (bf16[38,3,512]{2,1,0:T(4,128)(2,1)S(1)}, bf16[38,3,512]{2,1,0:T(4,128)(2,1)S(1)}, u32[]{:S(2)}, u32[]{:S(2)}) collective-permute-start(bf16[38,3,512]{2,1,0:T(4,128)(2,1)S(1)} %get-tuple-element.238), channel_id=1, source_target_pairs={{0,32},{32,64},{64,96},{1,33},{33,65},{65,97},{2,34},{34,66},{66,9... | collective-permute-start | bytes 350216 | tf_op jit(solution)/shard_map/ppermute | solution.py:27
  101.1 6.1 collective-permute-start.3
  104.4 16.5 %copy-start.6 = (bf16[2,64,8,32]{1,0,3,2:T(2,128)(2,1)}, bf16[2,64,8,32]{1,0,3,2:T(2,128)(2,1)S(1)}, u32[]{:S(2)}) copy-start(bf16[2,64,8,32]{1,0,3,2:T(2,128)(2,1)S(1)} %squeeze.40) | copy-start | bytes 196612
  105.2 0.7 copy-start.14
  115.9 2.1 copy-start.15
  115.9 2.8 copy-start.26
  117.8 3.1 copy-start.3
  118.7 1.8 copy-start.16
  118.7 1.8 copy-start.22
  120.5 1.3 copy-start.8
  123.2 1.2 copy-start.7
  132.9 13.1 %copy-start.10 = (bf16[128,256]{0,1:T(8,128)(2,1)S(1)}, bf16[128,256]{0,1:T(8,128)(2,1)}, u32[]{:S(2)}) copy-start(bf16[128,256]{0,1:T(8,128)(2,1)} %reshape.1063) | copy-start | bytes 196612
  132.9 13.1 %copy-start.17 = (bf16[1,1,1,128,512]{4,3,2,1,0:T(8,128)(2,1)S(1)}, bf16[1,1,1,128,512]{4,3,2,1,0:T(8,128)(2,1)}, u32[]{:S(2)}) copy-start(bf16[1,1,1,128,512]{4,3,2,1,0:T(8,128)(2,1)} %param.29) | copy-start | bytes 393220
  132.9 13.1 %copy-start.23 = (pred[128]{0:T(512)(128)(4,1)S(1)}, pred[128]{0:T(512)(128)(4,1)}, u32[]{:S(2)}) copy-start(pred[128]{0:T(512)(128)(4,1)} %broadcast_in_dim.150) | copy-start | bytes 388
  135.0 15.5 %collective-permute-start.4 = (bf16[3,38,512]{2,1,0:T(8,128)(2,1)S(1)}, bf16[3,38,512]{2,1,0:T(8,128)(2,1)S(1)}, u32[]{:S(2)}, u32[]{:S(2)}) collective-permute-start(bf16[3,38,512]{2,1,0:T(8,128)(2,1)S(1)} %get-tuple-element.236), channel_id=1, source_target_pairs={{0,128},{128,256},{256,384},{1,129},{129,257},{257,385},{2,130},{1... | collective-permute-start | bytes 350216 | tf_op jit(solution)/shard_map/ppermute | solution.py:27
  144.0 10.2 %collective-permute-start.5 = (bf16[3,38,512]{2,1,0:T(8,128)(2,1)S(1)}, bf16[3,38,512]{2,1,0:T(8,128)(2,1)S(1)}, u32[]{:S(2)}, u32[]{:S(2)}) collective-permute-start(bf16[3,38,512]{2,1,0:T(8,128)(2,1)S(1)} %get-tuple-element.237), channel_id=1, source_target_pairs={{128,0},{256,128},{384,256},{129,1},{257,129},{385,257},{130,2},{2... | collective-permute-start | bytes 350216 | tf_op jit(solution)/shard_map/ppermute | solution.py:28
  147.0 435.2 %reduce-scatter.3.cloned.1.call-start = ((), (), s32[]{:S(2)}) async-start(), calls=%async_computation.3 | async-start | bytes 811008 | tf_op jit(solution)/shard_map/reduce_scatter | solution.py:263
  150.5 10.3 %copy-start.4 = (bf16[2,196,256]{1,2,0:T(8,128)(2,1)S(1)}, bf16[2,196,256]{1,2,0:T(8,128)(2,1)}, u32[]{:S(2)}) copy-start(bf16[2,196,256]{1,2,0:T(8,128)(2,1)} %copy-done.3) | copy-start | bytes 602116
  155.0 7.0 %collective-permute-start.6 = (bf16[44,3,512]{2,1,0:T(4,128)(2,1)}, bf16[44,3,512]{2,1,0:T(4,128)(2,1)S(1)}, u32[]{:S(2)}, u32[]{:S(2)}) collective-permute-start(bf16[44,3,512]{2,1,0:T(4,128)(2,1)} %get-tuple-element.234), channel_id=1, source_target_pairs={{0,32},{32,64},{64,96},{1,33},{33,65},{65,97},{2,34},{34,66},{66,9... | collective-permute-start | bytes 405512 | tf_op jit(solution)/shard_map/ppermute | solution.py:27
  159.4 6.4 collective-permute-start.7
  189.3 4.0 copy-start.5
  189.3 4.0 copy-start.20
  190.8 3.9 copy-start.9
  192.6 3.0 copy-start.11
  192.6 3.0 copy-start.19
  193.3 4.4 copy-start.2
  194.7 100.0 %copy-start.24 = (f32[128]{0:T(128)S(1)}, f32[128]{0:T(128)}, u32[]{:S(2)}) copy-start(f32[128]{0:T(128)} %get-tuple-element.244) | copy-start | bytes 1540
Sparse Core Ops, SparseCore 0:
  147.1 211.7 reduce-scatter.4
  363.9 218.2 reduce-scatter.2
